TPU v7x, 128 devices: a whole 4x4x4 slice. The times are simulated.
128 devices in a mesh: mp: 8 (over z, x_lo), dp: 16 (over x_hi, y, core).
Axes of the slice: x: 4 (x_hi: 2, x_lo: 2; x = x_hi * 2 + x_lo), y: 4, z: 4, core: 2. Of those that a mesh axis runs over, the one named last changes fastest.
Arguments:
- volume: bfloat16 [16, 64, 64, 2048], P('dp', 'mp'), may hold values from -6 to 6
- kernel_a: bfloat16 [3, 3, 3, 32, 64], replicated, may hold values from -0.21875 to 0.21875
- kernel_b: bfloat16 [3, 3, 3, 64, 128], P(None, None, None, 'mp'), may hold values from -0.15625 to 0.15625
- cotangent: bfloat16 [16, 16, 16, 16, 128], P('dp', None, None, None, 'mp'), may hold values from -6 to 6
Outputs:
- features: bfloat16 [16, 16, 16, 16, 128], P('dp', None, None, None, 'mp')
- grad_a: float32 [3, 3, 3, 32, 64], replicated
- grad_b: float32 [3, 3, 3, 64, 128], P(None, None, None, 'mp')
All inputs are finite; a program needn't handle non-finite values.
Results may differ from a plain program's by a relative error of at most 0.0049.
Values may be sent and summed in bfloat16 or wider, within the bound.
A program may use at most 192 MiB of HBM per device.

v0:
```python
import math
import jax
import jax.numpy as jnp
from jax import lax
from jax.sharding import PartitionSpec as P

GRID = 64


def shifted(array, axis, by):
    size = lax.axis_size(axis)
    pairs = [(i, i + by) for i in range(size) if 0 <= i + by < size]
    return lax.ppermute(array, axis, pairs)


def forward_conv(padded, kernel):
    return lax.conv_general_dilated(
        padded,
        kernel,
        (2, 2, 2),
        "VALID",
        dimension_numbers=("NDHWC", "DHWIO", "NDHWC"),
        preferred_element_type=jnp.float32,
    )


def kernel_grad(padded, grads):
    result = lax.conv_general_dilated(
        padded,
        grads,
        (1, 1, 1),
        "VALID",
        rhs_dilation=(2, 2, 2),
        dimension_numbers=("CDHWN", "IDHWO", "NDHWC"),
        preferred_element_type=jnp.float32,
    )
    return jnp.transpose(result, (1, 2, 3, 0, 4))


def input_grad(grads, kernel, first_low):
    flipped = kernel[::-1, ::-1, ::-1]
    return lax.conv_general_dilated(
        grads,
        flipped,
        (1, 1, 1),
        ((first_low, 2), (1, 2), (1, 2)),
        lhs_dilation=(2, 2, 2),
        dimension_numbers=("NDHWC", "DHWOI", "NDHWC"),
        preferred_element_type=jnp.float32,
    )


def pad_sides(field):
    return jnp.pad(field, ((0, 0), (0, 0), (1, 0), (1, 0), (0, 0)))


def pad_low(field):
    return jnp.pad(field, ((0, 0), (1, 0), (1, 0), (1, 0), (0, 0)))


def shards(volume, kernel_a, kernel_b, cotangent):
    samp_local = volume.shape[0]
    planes = volume.shape[1]
    edge = volume.shape[2]
    in_chan = kernel_a.shape[3]
    field = volume.reshape(samp_local, planes, edge, edge, in_chan)
    below = shifted(field[:, planes - 1 :], "mp", 1)
    padded_x = pad_sides(jnp.concatenate([below, field], axis=1))
    pre = forward_conv(padded_x, kernel_a)
    hidden = jnp.where(pre > 0, pre, 0.3 * pre).astype(jnp.bfloat16)
    grouped = lax.all_to_all(hidden, "mp", split_axis=4, concat_axis=1, tiled=True)
    padded_h = pad_low(grouped)
    partial_out = forward_conv(padded_h, kernel_b)
    features = lax.psum_scatter(partial_out, "mp", scatter_dimension=4, tiled=True).astype(
        jnp.bfloat16
    )
    upstream = lax.all_gather(cotangent, "mp", axis=4, tiled=True)
    local_b = kernel_grad(padded_h, upstream)
    back_group = input_grad(upstream, kernel_b, 1).astype(jnp.bfloat16)
    back = lax.all_to_all(back_group, "mp", split_axis=1, concat_axis=4, tiled=True)
    delta = (back.astype(jnp.float32) * jnp.where(pre > 0, 1.0, 0.3)).astype(jnp.bfloat16)
    local_a = kernel_grad(padded_x, delta)
    total_a = lax.psum(local_a, ("mp", "dp"))
    total_b = lax.psum(local_b, "dp")
    samples_all = samp_local * lax.axis_size("dp")
    grad_a = total_a / math.sqrt(samples_all * (GRID // 2) ** 3)
    grad_b = total_b / math.sqrt(samples_all * (GRID // 4) ** 3)
    return (features, grad_a, grad_b)


def solution(mesh):
    return jax.shard_map(
        shards,
        mesh=mesh,
        in_specs=(
            P("dp", "mp", None, None),
            P(),
            P(None, None, None, "mp", None),
            P("dp", None, None, None, "mp"),
        ),
        out_specs=(P("dp", None, None, None, "mp"), P(), P(None, None, None, "mp", None)),
        check_vma=False,
    )
```

profile of v0, /device:TPU:1, one launch (start us, length us, event | category | flops | bytes accessed | tf_op | source)
XLA Modules:
  0.0 838.3 jit_solution(7763710412680146833)
XLA Ops:
  7.2 4.9 copy.124
  14.2 4.0 collective-permute-start
  18.2 31.5 %copy.127 = bf16[1,8,64,64,32]{4,0,3,2,1:T(2,128)(2,1)} copy(bf16[1,8,64,64,32]{2,4,3,1,0:T(8,128)(2,1)} %bitcast.69) | data formatting | bytes 4194304 | tf_op jit(solution)/shard_map/reshape | solution.py:66
  52.4 58.2 %pad_maximum_fusion = bf16[1,9,64,64,32]{4,0,3,2,1:T(2,128)(2,1)} fusion(bf16[1,8,64,64,32]{4,0,3,2,1:T(2,128)(2,1)} %copy.127, bf16[1,1,64,64,32]{4,0,3,2,1:T(2,128)(2,1)S(1)} %copy.126), kind=kLoop, calls=%fused_computation.4 | loop fusion | flops 1179648 | bytes 4718592 | tf_op jit(solution)/shard_map/concatenate | solution.py:68
  110.6 33.5 %copy.128 = bf16[1,9,64,64,32]{3,4,2,1,0:T(8,128)(2,1)} copy(bf16[1,9,64,64,32]{4,0,3,2,1:T(2,128)(2,1)} %pad_maximum_fusion) | data formatting | bytes 4718592 | tf_op jit(solution)/shard_map/concatenate | solution.py:68
  144.1 9.2 %copy.159 = bf16[9,64,1,64,32]{1,4,3,0,2:T(8,128)(2,1)} copy(bf16[9,64,1,64,32]{3,4,2,1,0:T(8,128)(2,1)} %bitcast.72) | data formatting | bytes 4718592
  153.3 6.1 pad.4.clone
  159.4 15.6 %copy.131 = bf16[9,64,1,8,10,32]{5,3,4,1,0,2:T(8,128)(2,1)} copy(bf16[9,64,1,8,10,32]{1,5,4,3,0,2:T(8,128)(2,1)} %bitcast.67) | data formatting | bytes 5898240 | tf_op jit(solution)/shard_map/conv_general_dilated | solution.py:17
  177.4 12.0 %compare_select_fusion = (f32[4,32,8,5,64]{4,2,3,1,0:T(8,128)}, bf16[4,32,8,5,64]{4,2,3,1,0:T(8,128)(2,1)S(1)}) fusion(pred[8,5]{0,1:T(8,128)(4,1)S(1)} %copy-done.6, bf16[3,3,3,32,64]{4,3,2,1,0:T(8,128)(2,1)S(1)} %copy-done, bf16[9,64,1,7,2,32]{5,3,4,1,0,2:T(8,128)(2,1)S(1)} %slice.12, bf16[9,64,1,8,10,32]{5,3,4,1,0,2:T(8,128)(2,1)} %copy.131), kind=kOutput, calls=%fused_computation.20 | convolution fusion | flops 572915712 | bytes 5541928 | tf_op jit(solution)/shard_map/conv_general_dilated | solution.py:17
  195.8 6.1 all-to-all-start
  202.0 3.9 copy.140
  216.9 3.4 copy.160
  220.4 4.0 pad.6.clone
  224.4 12.8 %copy.138 = bf16[32,32,1,8,6,8]{5,3,4,1,0,2:T(8,128)(2,1)} copy(bf16[32,32,1,8,6,8]{1,5,4,3,0,2:T(8,128)(2,1)} %bitcast.73) | data formatting | bytes 1572864 | tf_op jit(solution)/shard_map/conv_general_dilated | solution.py:17
  240.6 12.3 %broadcast_select_fusion = f32[16,16,8,3,128]{4,2,3,1,0:T(8,128)S(1)} fusion(pred[8,3]{0,1:T(4,128)(4,1)S(1)} %copy-done.7, bf16[3,3,3,8,128]{4,3,2,1,0:T(8,128)(2,1)S(1)} %copy-done.5, bf16[32,32,1,7,2,8]{5,3,4,1,0,2:T(8,128)(2,1)S(1)} %slice.14, bf16[32,32,1,8,6,8]{5,3,4,1,0,2:T(8,128)(2,1)} %copy.138), kind=kOutput, calls=%fused_computation.30 | convolution fusion | flops 329662464 | bytes 4216856 | tf_op jit(solution)/shard_map/conv_general_dilated | solution.py:17
  255.2 23.8 %copy.153 = bf16[1,32,32,32,8]{4,0,3,2,1:T(2,128)(2,1)} copy(bf16[1,32,32,32,8]{3,4,2,1,0:T(8,128)(2,1)S(1)} %bitcast.71) | data formatting | bytes 1048576 | tf_op jit(solution)/shard_map/all_to_all | solution.py:71
  279.0 97.7 %all-gather.2.cloned.1.call-done = bf16[1,16,16,16,128]{3,2,1,0,4:T(8,128)(2,1)} async-done(((bf16[1,16,16,16,16]{3,2,1,0,4:T(8,128)(2,1)}), bf16[1,16,16,16,128]{3,2,1,0,4:T(8,128)(2,1)}) %all-gather.2.cloned.1.call-update) | async-done | bytes 1048592 | tf_op jit(solution)/shard_map/all_gather | solution.py:77
  376.7 10.0 %copy.141 = bf16[1,16,16,16,128]{4,3,2,1,0:T(8,128)(2,1)S(1)} copy(bf16[1,16,16,16,128]{3,2,1,0,4:T(8,128)(2,1)} %all-gather.2.cloned.1.call-done) | data formatting | bytes 2097152 | tf_op jit(solution)/shard_map/all_gather | solution.py:77
  387.9 14.3 %fusion.17 = bf16[32,32,8,6,8]{4,2,3,1,0:T(8,128)(2,1)} fusion(bf16[3,3,3,8,128]{4,3,2,1,0:T(8,128)(2,1)S(1)} %copy-done.5, bf16[16,16,1,7,1,128]{5,3,4,1,0,2:T(8,128)(2,1)S(1)} %slice.16, bf16[16,16,1,8,3,128]{5,3,4,1,0,2:T(8,128)(2,1)S(1)} %copy.144), kind=kOutput, calls=%fused_computation.24 | convolution fusion | flops 332021760 | bytes 2873344 | tf_op jit(solution)/shard_map/conv_general_dilated | solution.py:42
  402.2 13.6 %copy.145 = bf16[32,32,8,6,8]{1,4,3,2,0:T(8,128)(2,1)S(1)} copy(bf16[32,32,8,6,8]{4,2,3,1,0:T(8,128)(2,1)} %fusion.17) | data formatting | bytes 1572864 | tf_op jit(solution)/shard_map/conv_general_dilated | solution.py:42
  419.7 4.9 all-to-all-start.1
  424.6 13.5 %copy.154 = bf16[1,16,16,16,128]{4,0,3,2,1:T(2,128)(2,1)S(1)} copy(bf16[1,16,16,16,128]{3,2,1,0,4:T(8,128)(2,1)} %all-gather.2.cloned.1.call-done) | data formatting | bytes 2097152 | tf_op jit(solution)/shard_map/all_gather | solution.py:77
  438.1 51.8 %fusion.36 = f32[3,3,3,8,128]{4,3,2,1,0:T(8,128)} fusion(bf16[1,32,32,32,8]{4,0,3,2,1:T(2,128)(2,1)} %copy.153, bf16[1,16,16,16,128]{4,0,3,2,1:T(2,128)(2,1)S(1)} %copy.154), kind=kOutput, calls=%fused_computation.46 | convolution fusion | flops 212629504 | bytes 1683456 | tf_op jit(solution)/shard_map/transpose | solution.py:37
  491.3 3.4 copy.147
  494.7 3.5 fusion.12
  498.2 4.1 copy.151
  502.3 46.6 %fusion.35 = f32[3,3,3,32,64]{4,3,2,1,0:T(8,128)} fusion(bf16[1,9,64,64,32]{4,0,3,2,1:T(2,128)(2,1)} %pad_maximum_fusion, bf16[1,4,32,32,64]{4,0,3,2,1:T(2,128)(2,1)} %copy.151), kind=kOutput, calls=%fused_computation.45 | convolution fusion | flops 443596800 | bytes 3104768 | tf_op jit(solution)/shard_map/transpose | solution.py:37
  550.5 14.3 %copy.156 = f32[1,16,16,16,128]{2,3,1,0,4:T(8,128)} copy(f32[1,16,16,16,128]{4,2,3,1,0:T(8,128)} %slice_bitcast_fusion.1) | data formatting | bytes 4194304
  564.8 15.3 %reshape.69 = f32[128,4096]{1,0:T(8,128)} reshape(f32[128,1,16,16,16]{4,3,2,1,0:T(8,128)} %bitcast.66) | data formatting | bytes 4194304
  580.1 45.1 %all-reduce.5.cloned.1.call-done = f32[3,3,3,8,128]{4,3,2,1,0:T(8,128)} async-done(((f32[3,3,3,8,128]{4,3,2,1,0:T(8,128)}), f32[3,3,3,8,128]{4,3,2,1,0:T(8,128)}) %all-reduce.5.cloned.1.call-update) | async-done | bytes 110608 | tf_op jit(solution)/shard_map/psum | solution.py:84
  626.8 147.3 %all-reduce.3.cloned.1.call-done = f32[3,3,3,32,64]{4,3,2,1,0:T(8,128)} async-done(((f32[3,3,3,32,64]{4,3,2,1,0:T(8,128)}), f32[3,3,3,32,64]{4,3,2,1,0:T(8,128)}) %all-reduce.3.cloned.1.call-update) | async-done | bytes 221200 | tf_op jit(solution)/shard_map/psum | solution.py:83
  775.9 51.3 %reduce-scatter.4.cloned.1.call-done = f32[16,4096]{1,0:T(8,128)} async-done(((f32[128,4096]{1,0:T(8,128)}), f32[16,4096]{1,0:T(8,128)}) %reduce-scatter.4.cloned.1.call-update) | async-done | bytes 262160
  (57 shorter events, 46.0 us)
Async XLA Ops:
  7.2 170.2 %copy-start = (bf16[3,3,3,32,64]{4,3,2,1,0:T(8,128)(2,1)S(1)}, bf16[3,3,3,32,64]{4,3,2,1,0:T(8,128)(2,1)}, u32[]{:S(2)}) copy-start(bf16[3,3,3,32,64]{4,3,2,1,0:T(8,128)(2,1)} %param.5) | copy-start | bytes 331780
  14.2 35.5 %collective-permute-start = (bf16[1,1,64,64,32]{3,4,2,1,0:T(8,128)(2,1)S(1)}, bf16[1,1,64,64,32]{3,4,2,1,0:T(8,128)(2,1)S(1)}, u32[]{:S(2)}, u32[]{:S(2)}) collective-permute-start(bf16[1,1,64,64,32]{3,4,2,1,0:T(8,128)(2,1)S(1)} %copy.125), channel_id=1, source_target_pairs={{0,16},{16,32},{32,48},{48,64},{64,80},{80,96},{96,112},{1,17},{17... | collective-permute-start | bytes 786440 | tf_op jit(solution)/shard_map/ppermute | solution.py:13
  175.0 2.4 copy-start.6
  195.8 10.1 %copy-start.3 = (f32[4,32,8,5,64]{4,2,3,1,0:T(8,128)S(1)}, f32[4,32,8,5,64]{4,2,3,1,0:T(8,128)}, u32[]{:S(2)}) copy-start(f32[4,32,8,5,64]{4,2,3,1,0:T(8,128)} %get-tuple-element.18) | copy-start | bytes 3932164
  195.8 15.0 %all-to-all-start = ((bf16[8,2,16384]{2,1,0:T(2,128)(2,1)}), bf16[8,2,16384]{2,1,0:T(2,128)(2,1)S(1)}, u32[]{:S(2)}, u32[]{:S(2)}) async-start(bf16[8,2,16384]{2,1,0:T(2,128)(2,1)} %reshape.71), calls=%async_computation | async-start | bytes 1048576 | tf_op jit(solution)/shard_map/all_to_all | solution.py:71
  202.0 174.8 %all-gather.2.cloned.1.call-start = ((), (), s32[]{:S(2)}) async-start(), calls=%async_computation.3 | async-start | bytes 9437184 | tf_op jit(solution)/shard_map/all_gather | solution.py:77
  237.2 3.4 copy-start.5
  237.2 3.5 copy-start.7
  402.2 13.6 %copy-start.4 = (pred[8,6]{1,0:T(8,128)(4,1)S(1)}, pred[8,6]{1,0:T(8,128)(4,1)}, u32[]{:S(2)}) copy-start(pred[8,6]{1,0:T(8,128)(4,1)} %constant.31) | copy-start | bytes 148
  419.7 70.3 %all-to-all-start.1 = ((bf16[8,2,16384]{2,1,0:T(2,128)(2,1)}), bf16[8,2,16384]{2,1,0:T(2,128)(2,1)S(1)}, u32[]{:S(2)}, u32[]{:S(2)}) async-start(bf16[8,2,16384]{2,1,0:T(2,128)(2,1)} %reshape.73), calls=%async_computation.1 | async-start | bytes 1048576 | tf_op jit(solution)/shard_map/all_to_all | solution.py:80
  424.6 200.6 %all-reduce.5.cloned.1.call-start = ((), (), s32[]{:S(2)}) async-start(), calls=%async_computation.5 | async-start | bytes 221184 | tf_op jit(solution)/shard_map/psum | solution.py:84
  489.9 284.1 %all-reduce.3.cloned.1.call-start = ((), (), s32[]{:S(2)}) async-start(), calls=%async_computation.4 | async-start | bytes 884736 | tf_op jit(solution)/shard_map/psum | solution.py:83
  502.3 46.7 %copy-start.2 = (f32[16,16,8,3,128]{4,1,3,2,0:T(8,128)S(1)}, f32[16,16,8,3,128]{4,1,3,2,0:T(8,128)}, u32[]{:S(2)}) copy-start(f32[16,16,8,3,128]{4,1,3,2,0:T(8,128)} %copy.139) | copy-start | bytes 9437188
  548.9 278.3 %reduce-scatter.4.cloned.1.call-start = ((), (), s32[]{:S(2)}) async-start(), calls=%async_computation.6 | async-start | bytes 2359296
  625.2 206.2 %copy-start.1 = (bf16[3,3,3,32,64]{4,3,2,1,0:T(8,128)(2,1)S(1)}, bf16[3,3,3,32,64]{4,3,2,1,0:T(8,128)(2,1)}, u32[]{:S(2)}) copy-start(bf16[3,3,3,32,64]{4,3,2,1,0:T(8,128)(2,1)} %param.5) | copy-start | bytes 331780
Sparse Core Ops, SparseCore 0:
  206.0 170.6 all-gather.1
  490.1 135.0 all-reduce.4
  631.2 142.7 all-reduce.2
  776.3 50.8 reduce-scatter.3
where the time goes:
time: 853 us; the launch traced here: 838 us
  waiting for transfers between devices  343 us (40%)
  local copies, waits for them, and re-layouts  263 us (31%)
  matrix products  137 us (16%)
  other arithmetic  66 us (8%)
  starting transfers between devices  15.2 us (2%)
  between operations  14.4 us (2%)
    psum x1, waiting for transfers between devices, shards(): total_a = lax.psum(local_a, ('mp', 'dp'))  147 us
    transpose x2, matrix products, kernel_grad(): return jnp.transpose(result, (1, 2, 3, 0, 4))  98.3 us
    all_gather x1, waiting for transfers between devices, shards(): upstream = lax.all_gather(cotangent, 'mp', axis=4, tiled=True)  97.7 us
    unnamed x32, local copies, waits for them, and re-layouts  66.3 us
    concatenate x1, other arithmetic, shards(): padded_x = pad_sides(jnp.concatenate([below, field], axis=1))  58.2 us
    unnamed x5, waiting for transfers between devices  51.4 us
    psum x1, waiting for transfers between devices, shards(): total_b = lax.psum(local_b, 'dp')  45.1 us
    concatenate x2, local copies, waits for them, and re-layouts, shards(): padded_x = pad_sides(jnp.concatenate([below, field], axis=1))  39.5 us
  transfers between devices with their start and end apart: 7, of which 5 were waited for; matrix products, arithmetic and copies ran while one was open for 32% of the time, Pallas kernels for 0%

commit v1 on v0

--- a/solution.py
+++ b/solution.py
@@ -5,6 +5,13 @@
 from jax.sharding import PartitionSpec as P
 
 GRID = 64
+
+
+def all_by_exchange(x, axis, along):
+    n_dev = lax.axis_size(axis)
+    blocks = jnp.stack([x for _ in range(n_dev)])
+    blocks = lax.all_to_all(blocks, axis, split_axis=0, concat_axis=0)
+    return jnp.concatenate(blocks, axis=along)
 
 
 def shifted(array, axis, by):
@@ -74,7 +81,7 @@
     features = lax.psum_scatter(partial_out, "mp", scatter_dimension=4, tiled=True).astype(
         jnp.bfloat16
     )
-    upstream = lax.all_gather(cotangent, "mp", axis=4, tiled=True)
+    upstream = all_by_exchange(cotangent, "mp", 4)
     local_b = kernel_grad(padded_h, upstream)
     back_group = input_grad(upstream, kernel_b, 1).astype(jnp.bfloat16)
     back = lax.all_to_all(back_group, "mp", split_axis=1, concat_axis=4, tiled=True)

time: 853 us -> 796 us (0.933)
  waiting for transfers between devices: 343 us -> 212 us
  local copies, waits for them, and re-layouts: 263 us -> 331 us
    all_gather x1 -> x0, waiting for transfers between devices: 97.7 us -> none  [shards(): upstream = lax.all_gather(cotangent, 'mp', axis=4, tiled=True)]
    reshape x0 -> x5, local copies, waits for them, and re-layouts: none -> 57 us  [all_by_exchange(): return jnp.concatenate(blocks, axis=along)]
    unnamed x5 -> x4, waiting for transfers between devices: 51.4 us -> 0.05 us
    unnamed x32 -> x34, local copies, waits for them, and re-layouts: 66.3 us -> 94.3 us
    all_gather x3 -> x0, local copies, waits for them, and re-layouts: 23.8 us -> none  [shards(): upstream = lax.all_gather(cotangent, 'mp', axis=4, tiled=True)]
    psum x1, waiting for transfers between devices: 45.1 us -> 56.5 us  [shards(): total_b = lax.psum(local_b, 'dp')]
  transfers between devices with their start and end apart: 7 -> 7, of which waited for: 5 -> 2; matrix products, arithmetic and copies ran while one was open for 32% -> 34% of each run, Pallas kernels for 0% -> 0%
where the time goes in v1:
time: 796 us; the launch traced here: 782 us
  local copies, waits for them, and re-layouts  331 us (42%)
  waiting for transfers between devices  212 us (27%)
  matrix products  137 us (17%)
  other arithmetic  66 us (8%)
  starting transfers between devices  20.3 us (3%)
  between operations  16.2 us (2%)
    psum x1, waiting for transfers between devices, shards(): total_a = lax.psum(local_a, ('mp', 'dp'))  155 us
    transpose x2, matrix products, kernel_grad(): return jnp.transpose(result, (1, 2, 3, 0, 4))  98.1 us
    unnamed x34, local copies, waits for them, and re-layouts  94.3 us
    concatenate x1, other arithmetic, shards(): padded_x = pad_sides(jnp.concatenate([below, field], axis=1))  58.2 us
    reshape x5, local copies, waits for them, and re-layouts, all_by_exchange(): return jnp.concatenate(blocks, axis=along)  57 us
    psum x1, waiting for transfers between devices, shards(): total_b = lax.psum(local_b, 'dp')  56.5 us
    concatenate x2, local copies, waits for them, and re-layouts, shards(): padded_x = pad_sides(jnp.concatenate([below, field], axis=1))  39.5 us
    conv_general_dilated x6, local copies, waits for them, and re-layouts, forward_conv(): lax.conv_general_dilated(padded, kernel, (2, 2, 2), 'VALID', dimension_nu...  38 us
  transfers between devices with their start and end apart: 7, of which 2 were waited for; matrix products, arithmetic and copies ran while one was open for 34% of the time, Pallas kernels for 0%

profile of v1, /device:TPU:1, one launch (start us, length us, event | category | flops | bytes accessed | tf_op | source)
XLA Modules:
  0.0 781.6 jit_solution(16233525691400242126)
XLA Ops:
  8.0 4.9 copy.121
  19.0 31.5 %copy.124 = bf16[1,8,64,64,32]{4,0,3,2,1:T(2,128)(2,1)} copy(bf16[1,8,64,64,32]{2,4,3,1,0:T(8,128)(2,1)} %bitcast.78) | data formatting | bytes 4194304 | tf_op jit(solution)/shard_map/reshape | solution.py:73
  53.2 58.2 %pad_maximum_fusion = bf16[1,9,64,64,32]{4,0,3,2,1:T(2,128)(2,1)} fusion(bf16[1,8,64,64,32]{4,0,3,2,1:T(2,128)(2,1)} %copy.124, bf16[1,1,64,64,32]{4,0,3,2,1:T(2,128)(2,1)S(1)} %copy.123), kind=kLoop, calls=%fused_computation.4 | loop fusion | flops 1179648 | bytes 4718592 | tf_op jit(solution)/shard_map/concatenate | solution.py:75
  111.5 33.5 %copy.125 = bf16[1,9,64,64,32]{3,4,2,1,0:T(8,128)(2,1)} copy(bf16[1,9,64,64,32]{4,0,3,2,1:T(2,128)(2,1)} %pad_maximum_fusion) | data formatting | bytes 4718592 | tf_op jit(solution)/shard_map/concatenate | solution.py:75
  144.9 9.2 %copy.155 = bf16[9,64,1,64,32]{1,4,3,0,2:T(8,128)(2,1)} copy(bf16[9,64,1,64,32]{3,4,2,1,0:T(8,128)(2,1)} %bitcast.81) | data formatting | bytes 4718592
  154.2 6.1 pad.4.clone
  160.2 15.6 %copy.128 = bf16[9,64,1,8,10,32]{5,3,4,1,0,2:T(8,128)(2,1)} copy(bf16[9,64,1,8,10,32]{1,5,4,3,0,2:T(8,128)(2,1)} %bitcast.76) | data formatting | bytes 5898240 | tf_op jit(solution)/shard_map/conv_general_dilated | solution.py:24
  178.2 12.0 %compare_select_fusion = (f32[4,32,8,5,64]{4,2,3,1,0:T(8,128)}, bf16[4,32,8,5,64]{4,2,3,1,0:T(8,128)(2,1)S(1)}) fusion(pred[8,5]{0,1:T(8,128)(4,1)S(1)} %copy-done.7, bf16[3,3,3,32,64]{4,3,2,1,0:T(8,128)(2,1)S(1)} %copy-done, bf16[9,64,1,7,2,32]{5,3,4,1,0,2:T(8,128)(2,1)S(1)} %slice.12, bf16[9,64,1,8,10,32]{5,3,4,1,0,2:T(8,128)(2,1)} %copy.128), kind=kOutput, calls=%fused_computation.20 | convolution fusion | flops 572915712 | bytes 5541928 | tf_op jit(solution)/shard_map/conv_general_dilated | solution.py:24
  193.9 12.8 %reshape.84 = bf16[8,2,16384]{2,1,0:T(2,128)(2,1)} reshape(bf16[64,1,4,32,32]{4,3,2,1,0:T(8,128)(2,1)S(1)} %bitcast.86) | data formatting | bytes 1048576
  206.7 5.9 all-to-all-start
  212.6 6.7 stack.2
  219.2 11.4 %reshape.86 = bf16[8,2,32768]{2,1,0:T(2,128)(2,1)} reshape(bf16[8,1,16,16,16,16]{5,4,3,2,1,0:T(8,128)(2,1)} %stack.2) | data formatting | bytes 2097152
  235.0 5.1 all-to-all-start.1
  251.7 4.0 pad.6.clone
  255.7 12.8 %copy.135 = bf16[32,32,1,8,6,8]{5,3,4,1,0,2:T(8,128)(2,1)} copy(bf16[32,32,1,8,6,8]{1,5,4,3,0,2:T(8,128)(2,1)} %bitcast.82) | data formatting | bytes 1572864 | tf_op jit(solution)/shard_map/conv_general_dilated | solution.py:24
  272.0 12.3 %broadcast_select_fusion = f32[16,16,8,3,128]{4,2,3,1,0:T(8,128)S(1)} fusion(pred[8,3]{0,1:T(4,128)(4,1)S(1)} %copy-done.8, bf16[3,3,3,8,128]{4,3,2,1,0:T(8,128)(2,1)S(1)} %copy-done.6, bf16[32,32,1,7,2,8]{5,3,4,1,0,2:T(8,128)(2,1)S(1)} %slice.14, bf16[32,32,1,8,6,8]{5,3,4,1,0,2:T(8,128)(2,1)} %copy.135), kind=kOutput, calls=%fused_computation.30 | convolution fusion | flops 329662464 | bytes 4216856 | tf_op jit(solution)/shard_map/conv_general_dilated | solution.py:24
  286.5 23.8 %copy.149 = bf16[1,32,32,32,8]{4,0,3,2,1:T(2,128)(2,1)} copy(bf16[1,32,32,32,8]{3,4,2,1,0:T(8,128)(2,1)S(1)} %bitcast.80) | data formatting | bytes 1048576 | tf_op jit(solution)/shard_map/all_to_all | solution.py:78
  310.2 7.8 %reshape.87 = bf16[8,1,16,16,16,16]{5,4,3,2,1,0:T(8,128)(2,1)} reshape(bf16[8,2,32768]{2,1,0:T(2,128)(2,1)S(1)} %all-to-all-done.1) | data formatting | bytes 2097152
  318.1 13.9 %copy.137 = bf16[1,16,16,16,8,16]{5,4,2,3,1,0:T(8,128)(2,1)} copy(bf16[1,16,16,16,8,16]{5,3,2,1,0,4:T(8,128)(2,1)} %bitcast.73) | data formatting | bytes 2097152 | tf_op jit(solution)/shard_map/reshape | solution.py:14
  331.9 20.2 %copy.148 = bf16[1,16,16,16,8,16]{5,4,3,2,1,0:T(8,128)(2,1)} copy(bf16[1,16,16,16,8,16]{5,3,2,1,0,4:T(8,128)(2,1)} %bitcast.74) | data formatting | bytes 2097152 | tf_op jit(solution)/shard_map/reshape | solution.py:14
  352.2 9.3 %reshape.71 = bf16[16,16,1,16,128]{4,1,3,0,2:T(8,128)(2,1)S(1)} reshape(bf16[1,16,16,16,8,16]{5,4,2,3,1,0:T(8,128)(2,1)} %copy.137) | data formatting | bytes 2097152 | tf_op jit(solution)/shard_map/reshape | solution.py:14
  361.4 13.3 %reshape.83 = bf16[1,16,16,16,128]{4,0,3,2,1:T(2,128)(2,1)} reshape(bf16[1,16,16,16,8,16]{5,4,3,2,1,0:T(8,128)(2,1)} %copy.148) | data formatting | bytes 2097152 | tf_op jit(solution)/shard_map/reshape | solution.py:14
  375.7 14.3 %fusion.17 = bf16[32,32,8,6,8]{4,2,3,1,0:T(8,128)(2,1)} fusion(bf16[3,3,3,8,128]{4,3,2,1,0:T(8,128)(2,1)S(1)} %copy-done.6, bf16[16,16,1,7,1,128]{5,3,4,1,0,2:T(8,128)(2,1)S(1)} %slice.16, bf16[16,16,1,8,3,128]{5,3,4,1,0,2:T(8,128)(2,1)S(1)} %copy.139), kind=kOutput, calls=%fused_computation.24 | convolution fusion | flops 332021760 | bytes 2873344 | tf_op jit(solution)/shard_map/conv_general_dilated | solution.py:49
  390.0 13.6 %copy.140 = bf16[32,32,8,6,8]{1,4,3,2,0:T(8,128)(2,1)S(1)} copy(bf16[32,32,8,6,8]{4,2,3,1,0:T(8,128)(2,1)} %fusion.17) | data formatting | bytes 1572864 | tf_op jit(solution)/shard_map/conv_general_dilated | solution.py:49
  407.5 5.1 all-to-all-start.2
  412.6 51.5 %fusion.36 = f32[3,3,3,8,128]{4,3,2,1,0:T(8,128)} fusion(bf16[1,32,32,32,8]{4,0,3,2,1:T(2,128)(2,1)} %copy.149, bf16[1,16,16,16,128]{4,0,3,2,1:T(2,128)(2,1)} %reshape.83), kind=kOutput, calls=%fused_computation.46 | convolution fusion | flops 212629504 | bytes 1683456 | tf_op jit(solution)/shard_map/transpose | solution.py:44
  472.5 4.1 copy.146
  476.6 46.6 %fusion.35 = f32[3,3,3,32,64]{4,3,2,1,0:T(8,128)} fusion(bf16[1,9,64,64,32]{4,0,3,2,1:T(2,128)(2,1)} %pad_maximum_fusion, bf16[1,4,32,32,64]{4,0,3,2,1:T(2,128)(2,1)} %copy.146), kind=kOutput, calls=%fused_computation.45 | convolution fusion | flops 443596800 | bytes 3104768 | tf_op jit(solution)/shard_map/transpose | solution.py:44
  524.8 14.3 %copy.152 = f32[1,16,16,16,128]{2,3,1,0,4:T(8,128)} copy(f32[1,16,16,16,128]{4,2,3,1,0:T(8,128)} %slice_bitcast_fusion.1) | data formatting | bytes 4194304
  539.1 15.3 %reshape.81 = f32[128,4096]{1,0:T(8,128)} reshape(f32[128,1,16,16,16]{4,3,2,1,0:T(8,128)} %bitcast.75) | data formatting | bytes 4194304
  554.4 56.5 %all-reduce.5.cloned.1.call-done = f32[3,3,3,8,128]{4,3,2,1,0:T(8,128)} async-done(((f32[3,3,3,8,128]{4,3,2,1,0:T(8,128)}), f32[3,3,3,8,128]{4,3,2,1,0:T(8,128)}) %all-reduce.5.cloned.1.call-update) | async-done | bytes 110608 | tf_op jit(solution)/shard_map/psum | solution.py:91
  612.5 155.2 %all-reduce.3.cloned.1.call-done = f32[3,3,3,32,64]{4,3,2,1,0:T(8,128)} async-done(((f32[3,3,3,32,64]{4,3,2,1,0:T(8,128)}), f32[3,3,3,32,64]{4,3,2,1,0:T(8,128)}) %all-reduce.3.cloned.1.call-update) | async-done | bytes 221200 | tf_op jit(solution)/shard_map/psum | solution.py:90
  (61 shorter events, 58.6 us)
Async XLA Ops:
  8.0 170.2 %copy-start = (bf16[3,3,3,32,64]{4,3,2,1,0:T(8,128)(2,1)S(1)}, bf16[3,3,3,32,64]{4,3,2,1,0:T(8,128)(2,1)}, u32[]{:S(2)}) copy-start(bf16[3,3,3,32,64]{4,3,2,1,0:T(8,128)(2,1)} %param.5) | copy-start | bytes 331780
  15.0 35.5 %collective-permute-start = (bf16[1,1,64,64,32]{3,4,2,1,0:T(8,128)(2,1)S(1)}, bf16[1,1,64,64,32]{3,4,2,1,0:T(8,128)(2,1)S(1)}, u32[]{:S(2)}, u32[]{:S(2)}) collective-permute-start(bf16[1,1,64,64,32]{3,4,2,1,0:T(8,128)(2,1)S(1)} %copy.122), channel_id=1, source_target_pairs={{0,16},{16,32},{32,48},{48,64},{64,80},{80,96},{96,112},{1,17},{17... | collective-permute-start | bytes 786440 | tf_op jit(solution)/shard_map/ppermute | solution.py:20
  175.9 2.4 copy-start.7
  206.7 27.5 %all-to-all-start = ((bf16[8,2,16384]{2,1,0:T(2,128)(2,1)}), bf16[8,2,16384]{2,1,0:T(2,128)(2,1)S(1)}, u32[]{:S(2)}, u32[]{:S(2)}) async-start(bf16[8,2,16384]{2,1,0:T(2,128)(2,1)} %reshape.84), calls=%async_computation | async-start | bytes 1048576 | tf_op jit(solution)/shard_map/all_to_all | solution.py:78
  219.2 11.4 %copy-start.3 = (f32[4,32,8,5,64]{4,2,3,1,0:T(8,128)S(1)}, f32[4,32,8,5,64]{4,2,3,1,0:T(8,128)}, u32[]{:S(2)}) copy-start(f32[4,32,8,5,64]{4,2,3,1,0:T(8,128)} %get-tuple-element.18) | copy-start | bytes 3932164
  234.2 0.8 copy-start.4
  235.0 75.2 %all-to-all-start.1 = ((bf16[8,2,32768]{2,1,0:T(2,128)(2,1)}), bf16[8,2,32768]{2,1,0:T(2,128)(2,1)S(1)}, u32[]{:S(2)}, u32[]{:S(2)}) async-start(bf16[8,2,32768]{2,1,0:T(2,128)(2,1)} %reshape.86), calls=%async_computation.1 | async-start | bytes 2097152 | tf_op jit(solution)/shard_map/all_to_all | solution.py:13
  268.5 3.4 copy-start.6
  268.5 3.4 copy-start.8
  390.0 13.6 %copy-start.5 = (pred[8,6]{1,0:T(8,128)(4,1)S(1)}, pred[8,6]{1,0:T(8,128)(4,1)}, u32[]{:S(2)}) copy-start(pred[8,6]{1,0:T(8,128)(4,1)} %constant.31) | copy-start | bytes 148
  407.5 56.8 %all-to-all-start.2 = ((bf16[8,2,16384]{2,1,0:T(2,128)(2,1)}), bf16[8,2,16384]{2,1,0:T(2,128)(2,1)S(1)}, u32[]{:S(2)}, u32[]{:S(2)}) async-start(bf16[8,2,16384]{2,1,0:T(2,128)(2,1)} %reshape.88), calls=%async_computation.2 | async-start | bytes 1048576 | tf_op jit(solution)/shard_map/all_to_all | solution.py:87
  412.6 198.3 %all-reduce.5.cloned.1.call-start = ((), (), s32[]{:S(2)}) async-start(), calls=%async_computation.5 | async-start | bytes 221184 | tf_op jit(solution)/shard_map/psum | solution.py:91
  464.2 303.5 %all-reduce.3.cloned.1.call-start = ((), (), s32[]{:S(2)}) async-start(), calls=%async_computation.4 | async-start | bytes 884736 | tf_op jit(solution)/shard_map/psum | solution.py:90
  476.5 46.7 %copy-start.2 = (f32[16,16,8,3,128]{4,1,3,2,0:T(8,128)S(1)}, f32[16,16,8,3,128]{4,1,3,2,0:T(8,128)}, u32[]{:S(2)}) copy-start(f32[16,16,8,3,128]{4,1,3,2,0:T(8,128)} %copy.136) | copy-start | bytes 9437188
  523.2 246.4 %reduce-scatter.4.cloned.1.call-start = ((), (), s32[]{:S(2)}) async-start(), calls=%async_computation.6 | async-start | bytes 2359296
  554.3 219.4 %copy-start.1 = (bf16[3,3,3,32,64]{4,3,2,1,0:T(8,128)(2,1)S(1)}, bf16[3,3,3,32,64]{4,3,2,1,0:T(8,128)(2,1)}, u32[]{:S(2)}) copy-start(bf16[3,3,3,32,64]{4,3,2,1,0:T(8,128)(2,1)} %param.5) | copy-start | bytes 331780
Sparse Core Ops, SparseCore 0:
  464.3 146.5 all-reduce.4
  617.0 150.6 all-reduce.2
Sparse Core Ops, SparseCore 1:
  554.5 55.8 reduce-scatter.3
